TPU v7x, 32 devices: a whole 2x2x4 slice. The times are simulated.
32 devices in a mesh: row: 4 (over y, core), col: 8 (over z, x).
Axes of the slice: x: 2, y: 2, z: 4, core: 2. Of those that a mesh axis runs over, the one named last changes fastest.
Arguments:
- row_gen: bfloat16 [64, 1024, 256], P(('row', 'col')), may hold values from -6 to 6
- row_upd: bfloat16 [64, 1024, 256], P(('row', 'col')), may hold values from -6 to 6
- col_gen: bfloat16 [64, 1024, 256], P('row', 'col'), may hold values from -6 to 6
- col_upd: bfloat16 [64, 1024, 256], P('row', 'col'), may hold values from -6 to 6
- leaf_rank: int32 [64], P(('row', 'col')), may hold values from 32 to 256, as said below
- leaf_trunc: int32 [64], P(('row', 'col')), may hold values from 128 to 512
- node_trunc: int32 [4, 14], replicated, may hold values from 128 to 384, as said below
- coupling: float32 [2048, 512], P(('row', 'col')), may hold values from -6 to 6
Outputs:
- recompressed: float32 [2048, 512], P(('row', 'col'))
Inputs may be any that keep to these rules, and one draw needn't show every extreme that they name: `leaf_rank`: the first leaf of every device (leaf indices that are multiples of 2) has rank 256. `node_trunc`: column 0 (the first height-0 node of each top node) is 384 in every row.
All inputs are finite; a program needn't handle non-finite values.
Results may differ from a plain program's by a relative error of at most 0.0003.
Values may be sent and summed in bfloat16 or wider, within the bound.
A program may use at most 128 MiB of HBM per device.

v0:
```python
import jax
import jax.numpy as jnp
from jax import lax
from jax.sharding import PartitionSpec as P

HIGH = lax.Precision.HIGHEST
OFFSETS = (0, 8, 12)


def partner(block, axis, distance):
    count = lax.axis_size(axis)
    route = []
    for low in range(count):
        high = low | 1 << distance
        if high != low and high < count:
            route += [(low, high), (high, low)]
    return lax.ppermute(block, axis, route)


def both_factors(generators, updates, ranks, truncs):
    leaf_count = ranks.shape[0] // 2
    width_gen = generators.shape[2]
    col_ids = lax.broadcasted_iota(jnp.int32, (1, 1, width_gen), 2)
    keep_cols = (col_ids < ranks[:, None, None]).astype(generators.dtype)
    stacked = jnp.concatenate([generators * keep_cols, updates], axis=2)
    gram_matrix = jnp.einsum("nlk,nlm->nkm", stacked, stacked, preferred_element_type=jnp.float32)
    width_all = gram_matrix.shape[1]
    gram_matrix = gram_matrix + jnp.eye(width_all, dtype=jnp.float32)
    factor = jnp.swapaxes(jnp.linalg.cholesky(gram_matrix), 1, 2)
    row_ids = lax.broadcasted_iota(jnp.int32, (1, width_all, 1), 1)
    kept_rows = factor * (row_ids < truncs[:, None, None]).astype(jnp.float32)
    kept_rows = kept_rows.reshape(2, leaf_count * width_all, width_all)
    node_gram = jnp.einsum("srk,srm->skm", kept_rows, kept_rows, precision=HIGH) + jnp.eye(
        width_all, dtype=jnp.float32
    )
    return jnp.swapaxes(jnp.linalg.cholesky(node_gram), 1, 2)


def truncate(factors, keep_rank):
    row_ids = lax.broadcasted_iota(jnp.int32, (1, factors.shape[1], 1), 1)
    return factors * (row_ids < keep_rank).astype(jnp.float32)


def merge_pair(own_rows, other_rows):
    width_all = own_rows.shape[2]
    gram_matrix = jnp.einsum("srk,srm->skm", own_rows, own_rows, precision=HIGH)
    gram_matrix = gram_matrix + jnp.einsum("srk,srm->skm", other_rows, other_rows, precision=HIGH)
    gram_matrix = gram_matrix + jnp.eye(width_all, dtype=jnp.float32)
    return jnp.swapaxes(jnp.linalg.cholesky(gram_matrix), 1, 2)


def body(row_gen, row_upd, col_gen, col_upd, leaf_rank, leaf_trunc, node_trunc, coupling):
    col_gen_full, col_upd_full = (
        lax.all_to_all(col_gen, "col", split_axis=0, concat_axis=1, tiled=True),
        lax.all_to_all(col_upd, "col", split_axis=0, concat_axis=1, tiled=True),
    )
    generators = jnp.concatenate([row_gen, col_gen_full], 0)
    updates = jnp.concatenate([row_upd, col_upd_full], 0)
    ranks = jnp.concatenate([leaf_rank, leaf_rank], 0)
    truncs = jnp.concatenate([leaf_trunc, leaf_trunc], 0)
    factors = both_factors(generators, updates, ranks, truncs)
    row_pos = lax.axis_index("row")
    col_pos = lax.axis_index("col")
    groups = lax.axis_size("col") // 8
    top_node = row_pos * groups + col_pos // 8
    member = col_pos % 8
    width_all = factors.shape[1]
    for height in range(3):
        keep_rank = node_trunc[top_node, OFFSETS[height] + (member >> height)]
        kept = truncate(factors, keep_rank)
        row_other, col_other = partner((kept[0], kept[1]), "col", height)
        factors = merge_pair(kept, jnp.stack([row_other, col_other], 0))
    row_factor = factors[0]
    col_factor = factors[1]
    partner_col = partner(col_factor, "row", 0)
    share_rows = width_all // 8
    my_rows = lax.dynamic_slice_in_dim(row_factor, member * share_rows, share_rows, 0)
    group_start = col_pos // 8 * width_all
    piece_rows = lax.all_gather(coupling, "col", axis=0, tiled=True)
    row_count = piece_rows.shape[0]
    positions = lax.broadcasted_iota(jnp.int32, (row_count,), 0) - group_start
    inside = (positions >= 0) & (positions < width_all)
    picked = jnp.take(my_rows, jnp.clip(positions, 0, width_all - 1), axis=1)
    picked = picked * inside.astype(jnp.float32)[None, :]
    projected = jnp.dot(picked, piece_rows, precision=HIGH)
    result = jnp.dot(projected, partner_col.T, precision=HIGH)
    return result / (8 * row_gen.shape[0] * row_gen.shape[1])


def solution(mesh):
    return jax.shard_map(
        body,
        mesh=mesh,
        in_specs=(
            P(("row", "col"), None, None),
            P(("row", "col"), None, None),
            P("row", "col", None),
            P("row", "col", None),
            P(("row", "col")),
            P(("row", "col")),
            P(),
            P(("row", "col"), None),
        ),
        out_specs=P(("row", "col"), None),
        check_vma=False,
    )
```

profile of v0, /device:TPU:1, one launch (start us, length us, event | category | flops | bytes accessed | tf_op | source)
XLA Modules:
  0.0 1381.0 jit_solution(1498919530769658933)
XLA Ops:
  6.5 31.4 %all_to_all.36 = bf16[16,128,256]{2,1,0:T(8,128)(2,1)} all-to-all(bf16[16,128,256]{2,1,0:T(8,128)(2,1)} %param.11), channel_id=1, replica_groups=mesh['row'=4,'col'=8] {'col'}, dimensions={0} | all-to-all | bytes 2097152 | tf_op jit(solution)/shard_map/all_to_all | solution.py:54
  37.9 4.2 all-to-all-start.1
  45.3 2.3 copy.130
  47.6 18.7 %all-to-all-done.1 = bf16[16,128,256]{2,1,0:T(8,128)(2,1)} async-done(((bf16[16,128,256]{2,1,0:T(8,128)(2,1)}), bf16[16,128,256]{2,1,0:T(8,128)(2,1)}, u32[]{:S(2)}, u32[]{:S(2)}) %all-to-all-start.1) | async-done | bytes 1048608 | tf_op jit(solution)/shard_map/all_to_all | solution.py:55
  69.3 4.7 fusion
  74.0 5.2 copy.134
  79.3 4.8 fusion.7
  86.0 46.9 %custom-call.55 = f32[4,128,128]{2,1,0:T(8,128)S(1)} custom-call(f32[4,128,128]{2,1,0:T(8,128)S(1)} %cholesky.1016), custom_call_target="Cholesky" | custom-call | tf_op jit(solution)/shard_map/jit(cholesky)/cholesky | solution.py:29
  132.9 39.3 %custom-call.56 = f32[4,1,128,128]{2,3,1,0:T(8,128)S(1)} custom-call(f32[4,1,128,128]{3,2,1,0:T(8,128)S(1)} %select_bitcast_fusion.3), custom_call_target="InvertDiagBlocksLowerTriangular" | custom-call | tf_op jit(solution)/shard_map/jit(cholesky)/cholesky | solution.py:29
  172.3 2.3 fusion.55
  174.8 2.6 convolution_subtract_fusion
  177.5 2.5 cholesky.240
  180.7 48.1 %custom-call.57 = f32[4,128,128]{2,1,0:T(8,128)S(1)} custom-call(f32[4,128,128]{2,1,0:T(8,128)} %cholesky.1020), custom_call_target="Cholesky" | custom-call | tf_op jit(solution)/shard_map/jit(cholesky)/cholesky | solution.py:29
  230.6 39.3 %custom-call.58 = f32[4,1,128,128]{2,3,1,0:T(8,128)S(1)} custom-call(f32[4,1,128,128]{3,2,1,0:T(8,128)S(1)} %get-tuple-element.37), custom_call_target="InvertDiagBlocksLowerTriangular" | custom-call | tf_op jit(solution)/shard_map/jit(cholesky)/cholesky | solution.py:29
  271.4 2.6 convolution_subtract_fusion.1
  274.0 46.9 %custom-call.59 = f32[4,128,128]{2,1,0:T(8,128)S(1)} custom-call(f32[4,128,128]{2,1,0:T(8,128)S(1)} %cholesky.1025), custom_call_target="Cholesky" | custom-call | tf_op jit(solution)/shard_map/jit(cholesky)/cholesky | solution.py:29
  321.7 39.5 %custom-call.60 = f32[4,1,128,128]{2,3,1,0:T(8,128)S(1)} custom-call(f32[4,1,128,128]{3,2,1,0:T(8,128)S(1)} %get-tuple-element.35), custom_call_target="InvertDiagBlocksLowerTriangular" | custom-call | tf_op jit(solution)/shard_map/jit(cholesky)/cholesky | solution.py:29
  362.3 2.6 convolution_subtract_fusion.10
  364.9 46.9 %custom-call.61 = f32[4,128,128]{2,1,0:T(8,128)S(1)} custom-call(f32[4,128,128]{2,1,0:T(8,128)S(1)} %convolution_subtract_fusion.10), custom_call_target="Cholesky" | custom-call | tf_op jit(solution)/shard_map/jit(cholesky)/cholesky | solution.py:29
  413.0 4.8 multiply_bitcast_fusion
  417.9 5.2 copy.146
  423.1 10.6 convolution_add_fusion
  439.0 23.5 %custom-call.83 = f32[2,128,128]{2,1,0:T(8,128)S(1)} custom-call(f32[2,128,128]{2,1,0:T(8,128)S(1)} %cholesky.1029), custom_call_target="Cholesky" | custom-call | tf_op jit(solution)/shard_map/jit(cholesky)/cholesky | solution.py:36
  463.4 21.1 %custom-call.84 = f32[2,1,128,128]{2,3,1,0:T(8,128)} custom-call(f32[2,1,128,128]{3,2,1,0:T(8,128)} %select_bitcast_fusion.15), custom_call_target="InvertDiagBlocksLowerTriangular" | custom-call | tf_op jit(solution)/shard_map/jit(cholesky)/cholesky | solution.py:36
  489.0 25.3 %custom-call.85 = f32[2,128,128]{2,1,0:T(8,128)} custom-call(f32[2,128,128]{2,1,0:T(8,128)} %cholesky.1033), custom_call_target="Cholesky" | custom-call | tf_op jit(solution)/shard_map/jit(cholesky)/cholesky | solution.py:36
  515.8 21.1 %custom-call.86 = f32[2,1,128,128]{2,3,1,0:T(8,128)} custom-call(f32[2,1,128,128]{3,2,1,0:T(8,128)} %get-tuple-element.57), custom_call_target="InvertDiagBlocksLowerTriangular" | custom-call | tf_op jit(solution)/shard_map/jit(cholesky)/cholesky | solution.py:36
  541.3 24.9 %custom-call.87 = f32[2,128,128]{2,1,0:T(8,128)} custom-call(f32[2,128,128]{2,1,0:T(8,128)} %cholesky.1038), custom_call_target="Cholesky" | custom-call | tf_op jit(solution)/shard_map/jit(cholesky)/cholesky | solution.py:36
  567.7 21.2 %custom-call.88 = f32[2,1,128,128]{2,3,1,0:T(8,128)} custom-call(f32[2,1,128,128]{3,2,1,0:T(8,128)} %get-tuple-element.55), custom_call_target="InvertDiagBlocksLowerTriangular" | custom-call | tf_op jit(solution)/shard_map/jit(cholesky)/cholesky | solution.py:36
  592.4 25.1 %custom-call.89 = f32[2,128,128]{2,1,0:T(8,128)} custom-call(f32[2,128,128]{2,1,0:T(8,128)} %convolution_subtract_fusion.14), custom_call_target="Cholesky" | custom-call | tf_op jit(solution)/shard_map/jit(cholesky)/cholesky | solution.py:36
  620.3 2.3 collective-permute-start
  624.0 4.3 fusion.25
  628.3 15.6 %collective-permute-done = f32[512,512]{0,1:T(8,128)S(1)} collective-permute-done((f32[512,512]{0,1:T(8,128)S(1)}, f32[512,512]{0,1:T(8,128)S(1)}, u32[]{:S(2)}, u32[]{:S(2)}) %collective-permute-start) | collective-permute-done | bytes 1048608 | tf_op jit(solution)/shard_map/ppermute | solution.py:17
  643.9 22.5 %collective-permute-done.1 = f32[512,512]{0,1:T(8,128)S(1)} collective-permute-done((f32[512,512]{0,1:T(8,128)S(1)}, f32[512,512]{0,1:T(8,128)S(1)}, u32[]{:S(2)}, u32[]{:S(2)}) %collective-permute-start.1) | collective-permute-done | bytes 1048608 | tf_op jit(solution)/shard_map/ppermute | solution.py:17
  666.3 3.5 add_add_fusion.2
  675.2 23.9 %custom-call.90 = f32[2,128,128]{2,1,0:T(8,128)S(1)} custom-call(f32[2,128,128]{2,1,0:T(8,128)S(1)} %cholesky.1042), custom_call_target="Cholesky" | custom-call | tf_op jit(solution)/shard_map/jit(cholesky)/cholesky | solution.py:49
  700.0 21.1 %custom-call.91 = f32[2,1,128,128]{2,3,1,0:T(8,128)} custom-call(f32[2,1,128,128]{3,2,1,0:T(8,128)} %select_bitcast_fusion.12), custom_call_target="InvertDiagBlocksLowerTriangular" | custom-call | tf_op jit(solution)/shard_map/jit(cholesky)/cholesky | solution.py:49
  725.6 24.9 %custom-call.92 = f32[2,128,128]{2,1,0:T(8,128)} custom-call(f32[2,128,128]{2,1,0:T(8,128)} %cholesky.1046), custom_call_target="Cholesky" | custom-call | tf_op jit(solution)/shard_map/jit(cholesky)/cholesky | solution.py:49
  752.0 21.2 %custom-call.93 = f32[2,1,128,128]{2,3,1,0:T(8,128)} custom-call(f32[2,1,128,128]{3,2,1,0:T(8,128)} %get-tuple-element.52), custom_call_target="InvertDiagBlocksLowerTriangular" | custom-call | tf_op jit(solution)/shard_map/jit(cholesky)/cholesky | solution.py:49
  777.6 24.9 %custom-call.94 = f32[2,128,128]{2,1,0:T(8,128)} custom-call(f32[2,128,128]{2,1,0:T(8,128)} %cholesky.1051), custom_call_target="Cholesky" | custom-call | tf_op jit(solution)/shard_map/jit(cholesky)/cholesky | solution.py:49
  804.1 21.1 %custom-call.95 = f32[2,1,128,128]{2,3,1,0:T(8,128)} custom-call(f32[2,1,128,128]{3,2,1,0:T(8,128)} %get-tuple-element.50), custom_call_target="InvertDiagBlocksLowerTriangular" | custom-call | tf_op jit(solution)/shard_map/jit(cholesky)/cholesky | solution.py:49
  828.6 25.1 %custom-call.96 = f32[2,128,128]{2,1,0:T(8,128)} custom-call(f32[2,128,128]{2,1,0:T(8,128)} %convolution_subtract_fusion.13), custom_call_target="Cholesky" | custom-call | tf_op jit(solution)/shard_map/jit(cholesky)/cholesky | solution.py:49
  859.3 4.3 fusion.27
  863.5 14.8 %collective-permute-done.2 = f32[512,512]{0,1:T(8,128)S(1)} collective-permute-done((f32[512,512]{0,1:T(8,128)S(1)}, f32[512,512]{0,1:T(8,128)S(1)}, u32[]{:S(2)}, u32[]{:S(2)}) %collective-permute-start.2) | collective-permute-done | bytes 1048608 | tf_op jit(solution)/shard_map/ppermute | solution.py:17
  878.3 22.5 %collective-permute-done.3 = f32[512,512]{0,1:T(8,128)S(1)} collective-permute-done((f32[512,512]{0,1:T(8,128)S(1)}, f32[512,512]{0,1:T(8,128)S(1)}, u32[]{:S(2)}, u32[]{:S(2)}) %collective-permute-start.3) | collective-permute-done | bytes 1048608 | tf_op jit(solution)/shard_map/ppermute | solution.py:17
  900.8 3.5 add_add_fusion.1
  909.7 23.9 %custom-call.97 = f32[2,128,128]{2,1,0:T(8,128)S(1)} custom-call(f32[2,128,128]{2,1,0:T(8,128)S(1)} %cholesky.1055), custom_call_target="Cholesky" | custom-call | tf_op jit(solution)/shard_map/jit(cholesky)/cholesky | solution.py:49
  934.5 21.1 %custom-call.98 = f32[2,1,128,128]{2,3,1,0:T(8,128)} custom-call(f32[2,1,128,128]{3,2,1,0:T(8,128)} %select_bitcast_fusion.9), custom_call_target="InvertDiagBlocksLowerTriangular" | custom-call | tf_op jit(solution)/shard_map/jit(cholesky)/cholesky | solution.py:49
  960.0 24.9 %custom-call.99 = f32[2,128,128]{2,1,0:T(8,128)} custom-call(f32[2,128,128]{2,1,0:T(8,128)} %cholesky.1059), custom_call_target="Cholesky" | custom-call | tf_op jit(solution)/shard_map/jit(cholesky)/cholesky | solution.py:49
  986.5 21.2 %custom-call.100 = f32[2,1,128,128]{2,3,1,0:T(8,128)} custom-call(f32[2,1,128,128]{3,2,1,0:T(8,128)} %get-tuple-element.47), custom_call_target="InvertDiagBlocksLowerTriangular" | custom-call | tf_op jit(solution)/shard_map/jit(cholesky)/cholesky | solution.py:49
  1012.1 24.9 %custom-call.101 = f32[2,128,128]{2,1,0:T(8,128)} custom-call(f32[2,128,128]{2,1,0:T(8,128)} %cholesky.1064), custom_call_target="Cholesky" | custom-call | tf_op jit(solution)/shard_map/jit(cholesky)/cholesky | solution.py:49
  1038.5 21.1 %custom-call.102 = f32[2,1,128,128]{2,3,1,0:T(8,128)} custom-call(f32[2,1,128,128]{3,2,1,0:T(8,128)} %get-tuple-element.45), custom_call_target="InvertDiagBlocksLowerTriangular" | custom-call | tf_op jit(solution)/shard_map/jit(cholesky)/cholesky | solution.py:49
  1063.1 25.1 %custom-call.103 = f32[2,128,128]{2,1,0:T(8,128)} custom-call(f32[2,128,128]{2,1,0:T(8,128)} %convolution_subtract_fusion.12), custom_call_target="Cholesky" | custom-call | tf_op jit(solution)/shard_map/jit(cholesky)/cholesky | solution.py:49
  1092.3 4.3 collective-permute-start.4
  1096.7 4.3 fusion.29
  1100.9 67.8 %collective-permute-done.4 = f32[512,512]{0,1:T(8,128)} collective-permute-done((f32[512,512]{0,1:T(8,128)}, f32[512,512]{0,1:T(8,128)}, u32[]{:S(2)}, u32[]{:S(2)}) %collective-permute-start.4) | collective-permute-done | bytes 1048608 | tf_op jit(solution)/shard_map/ppermute | solution.py:17
  1168.7 22.5 %collective-permute-done.5 = f32[512,512]{0,1:T(8,128)} collective-permute-done((f32[512,512]{0,1:T(8,128)}, f32[512,512]{0,1:T(8,128)}, u32[]{:S(2)}, u32[]{:S(2)}) %collective-permute-start.5) | collective-permute-done | bytes 1048608 | tf_op jit(solution)/shard_map/ppermute | solution.py:17
  1191.2 5.8 add_add_fusion
  1202.5 23.9 %custom-call.104 = f32[2,128,128]{2,1,0:T(8,128)S(1)} custom-call(f32[2,128,128]{2,1,0:T(8,128)S(1)} %cholesky.1068), custom_call_target="Cholesky" | custom-call | tf_op jit(solution)/shard_map/jit(cholesky)/cholesky | solution.py:49
  1226.6 19.7 %custom-call.105 = f32[2,1,128,128]{2,3,1,0:T(8,128)S(1)} custom-call(f32[2,1,128,128]{3,2,1,0:T(8,128)S(1)} %select_bitcast_fusion.6), custom_call_target="InvertDiagBlocksLowerTriangular" | custom-call | tf_op jit(solution)/shard_map/jit(cholesky)/cholesky | solution.py:49
  1250.7 23.5 %custom-call.106 = f32[2,128,128]{2,1,0:T(8,128)S(1)} custom-call(f32[2,128,128]{2,1,0:T(8,128)S(1)} %cholesky.1072), custom_call_target="Cholesky" | custom-call | tf_op jit(solution)/shard_map/jit(cholesky)/cholesky | solution.py:49
  1274.3 19.8 %custom-call.107 = f32[2,1,128,128]{2,3,1,0:T(8,128)S(1)} custom-call(f32[2,1,128,128]{3,2,1,0:T(8,128)S(1)} %get-tuple-element.42), custom_call_target="InvertDiagBlocksLowerTriangular" | custom-call | tf_op jit(solution)/shard_map/jit(cholesky)/cholesky | solution.py:49
  1297.1 23.5 %custom-call.108 = f32[2,128,128]{2,1,0:T(8,128)S(1)} custom-call(f32[2,128,128]{2,1,0:T(8,128)S(1)} %cholesky.1077), custom_call_target="Cholesky" | custom-call | tf_op jit(solution)/shard_map/jit(cholesky)/cholesky | solution.py:49
  1320.5 19.7 %custom-call.109 = f32[2,1,128,128]{2,3,1,0:T(8,128)S(1)} custom-call(f32[2,1,128,128]{3,2,1,0:T(8,128)S(1)} %get-tuple-element.40), custom_call_target="InvertDiagBlocksLowerTriangular" | custom-call | tf_op jit(solution)/shard_map/jit(cholesky)/cholesky | solution.py:49
  1342.0 23.7 %custom-call.110 = f32[2,128,128]{2,1,0:T(8,128)S(1)} custom-call(f32[2,128,128]{2,1,0:T(8,128)S(1)} %convolution_subtract_fusion.11), custom_call_target="Cholesky" | custom-call | tf_op jit(solution)/shard_map/jit(cholesky)/cholesky | solution.py:49
  (190 shorter events, 117.0 us)
Async XLA Ops:
  37.9 28.4 %all-to-all-start.1 = ((bf16[16,128,256]{2,1,0:T(8,128)(2,1)}), bf16[16,128,256]{2,1,0:T(8,128)(2,1)}, u32[]{:S(2)}, u32[]{:S(2)}) async-start(bf16[16,128,256]{2,1,0:T(8,128)(2,1)} %param.12), calls=%async_computation.1 | async-start | bytes 2097152 | tf_op jit(solution)/shard_map/all_to_all | solution.py:55
  42.2 0.7 copy-start.21
  42.2 1.3 copy-start.23
  42.2 1.4 copy-start.24
  42.2 1328.2 %all-gather.2.cloned.1.call-start = ((), (), s32[]{:S(2)}) async-start(), calls=%async_computation.2 | async-start | bytes 1179648 | tf_op jit(solution)/shard_map/all_gather | solution.py:79
  44.9 366.9 %copy-start.16 = (pred[128,128]{1,0:T(8,128)(4,1)}, pred[128,128]{1,0:T(8,128)(4,1)S(1)}, u32[]{:S(2)}) copy-start(pred[128,128]{1,0:T(8,128)(4,1)S(1)} %iota_compare_fusion.3) | copy-start | bytes 49156
  66.3 1.5 copy-start.5
  66.3 1.9 copy-start.15
  68.1 1.2 copy-start.22
  84.0 1.9 copy-start
  177.4 2.5 copy-start.6
  180.7 89.2 %copy-start.7 = (f32[4,384,128]{2,1,0:T(8,128)S(1)}, f32[4,384,128]{2,1,0:T(8,128)}, u32[]{:S(2)}) copy-start(f32[4,384,128]{2,1,0:T(8,128)} %copy-done.6) | copy-start | bytes 2359300
  437.7 1.4 copy-start.2
  487.6 0.8 copy-start.9
  539.9 0.7 copy-start.12
  620.1 3.9 copy-start.18
  620.3 23.5 %collective-permute-start = (f32[512,512]{0,1:T(8,128)S(1)}, f32[512,512]{0,1:T(8,128)S(1)}, u32[]{:S(2)}, u32[]{:S(2)}) collective-permute-start(f32[512,512]{0,1:T(8,128)S(1)} %get-tuple-element.32), channel_id=1, source_target_pairs={{0,1},{1,0},{2,3},{3,2},{4,5},{5,4},{6,7},{7,6},{8,9},{9,8},{10,11... | collective-permute-start | bytes 3145736 | tf_op jit(solution)/shard_map/ppermute | solution.py:17
  622.7 43.7 %collective-permute-start.1 = (f32[512,512]{0,1:T(8,128)S(1)}, f32[512,512]{0,1:T(8,128)S(1)}, u32[]{:S(2)}, u32[]{:S(2)}) collective-permute-start(f32[512,512]{0,1:T(8,128)S(1)} %get-tuple-element.33), channel_id=1, source_target_pairs={{0,1},{1,0},{2,3},{3,2},{4,5},{5,4},{6,7},{7,6},{8,9},{9,8},{10,11... | collective-permute-start | bytes 3145736 | tf_op jit(solution)/shard_map/ppermute | solution.py:17
  673.9 1.4 copy-start.3
  724.1 0.8 copy-start.10
  776.2 0.7 copy-start.13
  856.3 2.9 copy-start.20
  856.5 21.8 %collective-permute-start.2 = (f32[512,512]{0,1:T(8,128)S(1)}, f32[512,512]{0,1:T(8,128)S(1)}, u32[]{:S(2)}, u32[]{:S(2)}) collective-permute-start(f32[512,512]{0,1:T(8,128)S(1)} %get-tuple-element.30), channel_id=1, source_target_pairs={{0,2},{2,0},{1,3},{3,1},{4,6},{6,4},{5,7},{7,5},{8,10},{10,8},{9,1... | collective-permute-start | bytes 3145736 | tf_op jit(solution)/shard_map/ppermute | solution.py:17
  856.7 44.1 %collective-permute-start.3 = (f32[512,512]{0,1:T(8,128)S(1)}, f32[512,512]{0,1:T(8,128)S(1)}, u32[]{:S(2)}, u32[]{:S(2)}) collective-permute-start(f32[512,512]{0,1:T(8,128)S(1)} %get-tuple-element.31), channel_id=1, source_target_pairs={{0,2},{2,0},{1,3},{3,1},{4,6},{6,4},{5,7},{7,5},{8,10},{10,8},{9,1... | collective-permute-start | bytes 3145736 | tf_op jit(solution)/shard_map/ppermute | solution.py:17
  908.3 1.4 copy-start.4
  958.6 0.8 copy-start.11
  1010.7 0.7 copy-start.14
  1090.8 5.9 copy-start.19
  1092.3 76.4 %collective-permute-start.4 = (f32[512,512]{0,1:T(8,128)}, f32[512,512]{0,1:T(8,128)}, u32[]{:S(2)}, u32[]{:S(2)}) collective-permute-start(f32[512,512]{0,1:T(8,128)} %get-tuple-element.28), channel_id=1, source_target_pairs={{0,4},{4,0},{1,5},{5,1},{2,6},{6,2},{3,7},{7,3},{8,12},{12,8},{9,1... | collective-permute-start | bytes 3145736 | tf_op jit(solution)/shard_map/ppermute | solution.py:17
  1096.6 94.6 %collective-permute-start.5 = (f32[512,512]{0,1:T(8,128)}, f32[512,512]{0,1:T(8,128)}, u32[]{:S(2)}, u32[]{:S(2)}) collective-permute-start(f32[512,512]{0,1:T(8,128)} %get-tuple-element.29), channel_id=1, source_target_pairs={{0,4},{4,0},{1,5},{5,1},{2,6},{6,2},{3,7},{7,3},{8,12},{12,8},{9,1... | collective-permute-start | bytes 3145736 | tf_op jit(solution)/shard_map/ppermute | solution.py:17
  1201.1 1.4 copy-start.1
  1250.0 0.7 copy-start.8
  1274.2 91.5 %copy-start.17 = (pred[128,128]{1,0:T(8,128)(4,1)S(1)}, pred[128,128]{1,0:T(8,128)(4,1)}, u32[]{:S(2)}) copy-start(pred[128,128]{1,0:T(8,128)(4,1)} %copy-done.16) | copy-start | bytes 49156
  1367.8 4.7 collective-permute-start.6
Sparse Core Ops, SparseCore 0:
  1096.8 116.9 all-gather.1
where the time goes:
time: 1390 us; the launch traced here: 1380 us
  other arithmetic  993 us (71%)
  waiting for transfers between devices  184 us (13%)
  matrix products  93.4 us (7%)
  local copies, waits for them, and re-layouts  50.8 us (4%)
  blocking collectives  31.4 us (2%)
  between operations  14.6 us (1%)
  starting transfers between devices  13.9 us (1%)
    another operation x49, other arithmetic, merge_pair(): return jnp.swapaxes(jnp.linalg.cholesky(gram_matrix), 1, 2)  489 us
    another operation x15, other arithmetic, both_factors(): factor = jnp.swapaxes(jnp.linalg.cholesky(gram_matrix), 1, 2)  310 us
    another operation x16, other arithmetic, both_factors(): return jnp.swapaxes(jnp.linalg.cholesky(node_gram), 1, 2)  168 us
    ppermute x7, waiting for transfers between devices, partner(): return lax.ppermute(block, axis, route)  166 us
    all_to_all x1, blocking collectives, body(): lax.all_to_all(col_gen, 'col', split_axis=0, concat_axis=1, tiled=True)  31.4 us
  transfers between devices with their start and end apart: 9, of which 7 were waited for; matrix products, arithmetic and copies ran while one was open for 14% of the time, Pallas kernels for 0%

commit v1 on v0

--- a/solution.py
+++ b/solution.py
@@ -5,6 +5,28 @@
 
 HIGH = lax.Precision.HIGHEST
 OFFSETS = (0, 8, 12)
+
+
+def in_blocks(x, dim, devices):
+    before, after = (x.shape[:dim], x.shape[dim + 1 :])
+    return jnp.moveaxis(x.reshape(*before, devices, -1, *after), dim, 0)
+
+
+def in_order(parts, dim):
+    dims = list(parts.shape[1:])
+    dims[dim] *= parts.shape[0]
+    return jnp.moveaxis(parts, 0, dim).reshape(dims)
+
+
+def exchange_in_pairs(x, axis, split_dim, concat_dim):
+    size, place = (lax.axis_size(axis), lax.axis_index(axis))
+    blocks = in_blocks(x, split_dim, size)
+    outs = [blocks[place]]
+    for lap in range(1, size):
+        sent = blocks[place ^ lap]
+        outs.append(lax.ppermute(sent, axis, [(i, i ^ lap) for i in range(size)]))
+    blocks = jnp.stack(outs)[place ^ jnp.arange(size)]
+    return in_order(blocks, concat_dim)
 
 
 def partner(block, axis, distance):
@@ -51,7 +73,7 @@
 
 def body(row_gen, row_upd, col_gen, col_upd, leaf_rank, leaf_trunc, node_trunc, coupling):
     col_gen_full, col_upd_full = (
-        lax.all_to_all(col_gen, "col", split_axis=0, concat_axis=1, tiled=True),
+        exchange_in_pairs(col_gen, "col", 0, 1),
         lax.all_to_all(col_upd, "col", split_axis=0, concat_axis=1, tiled=True),
     )
     generators = jnp.concatenate([row_gen, col_gen_full], 0)

time: 1390 us -> 1390 us (level)
  blocking collectives: 31.4 us -> 0 us
  starting transfers between devices: 13.9 us -> 34.7 us
    all_to_all x1 -> x0, blocking collectives: 31.4 us -> none  [body(): lax.all_to_all(col_gen, 'col', split_axis=0, concat_axis=1, tiled=True)]
    all_to_all x1, waiting for transfers between devices: 18.7 us -> 1.05 us  [body(): lax.all_to_all(col_upd, 'col', split_axis=0, concat_axis=1, tiled=True)]
    another operation x15 -> x17, other arithmetic: 310 us -> 310 us  [both_factors(): factor = jnp.swapaxes(jnp.linalg.cholesky(gram_matrix), 1, 2)]
  transfers between devices with their start and end apart: 9 -> 16, of which waited for: 7 -> 9; matrix products, arithmetic and copies ran while one was open for 14% -> 15% of each run, Pallas kernels for 0% -> 0%
where the time goes in v1:
time: 1390 us; the launch traced here: 1380 us
  other arithmetic  994 us (72%)
  waiting for transfers between devices  179 us (13%)
  matrix products  94.6 us (7%)
  local copies, waits for them, and re-layouts  63.4 us (5%)
  starting transfers between devices  34.7 us (2%)
  between operations  14.6 us (1%)
    another operation x49, other arithmetic, merge_pair(): return jnp.swapaxes(jnp.linalg.cholesky(gram_matrix), 1, 2)  489 us
    another operation x17, other arithmetic, both_factors(): factor = jnp.swapaxes(jnp.linalg.cholesky(gram_matrix), 1, 2)  310 us
    another operation x16, other arithmetic, both_factors(): return jnp.swapaxes(jnp.linalg.cholesky(node_gram), 1, 2)  168 us
    ppermute x7, waiting for transfers between devices, partner(): return lax.ppermute(block, axis, route)  167 us
  transfers between devices with their start and end apart: 16, of which 9 were waited for; matrix products, arithmetic and copies ran while one was open for 15% of the time, Pallas kernels for 0%

profile of v1, /device:TPU:1, one launch (start us, length us, event | category | flops | bytes accessed | tf_op | source)
XLA Modules:
  0.0 1380.8 jit_solution(10003636659192546869)
XLA Ops:
  12.2 2.4 collective-permute-start.3
  15.6 4.6 all-to-all-start
  23.1 3.3 collective-permute-start.5
  35.4 10.0 collective-permute-done.5
  48.4 2.9 gather_fusion
  57.3 5.9 fusion
  63.2 5.5 copy.133
  68.7 4.8 fusion.7
  75.5 46.9 %custom-call.55 = f32[4,128,128]{2,1,0:T(8,128)S(1)} custom-call(f32[4,128,128]{2,1,0:T(8,128)S(1)} %cholesky.1016), custom_call_target="Cholesky" | custom-call | tf_op jit(solution)/shard_map/jit(cholesky)/cholesky | solution.py:51
  122.4 39.3 %custom-call.56 = f32[4,1,128,128]{2,3,1,0:T(8,128)S(1)} custom-call(f32[4,1,128,128]{3,2,1,0:T(8,128)S(1)} %select_bitcast_fusion.3), custom_call_target="InvertDiagBlocksLowerTriangular" | custom-call | tf_op jit(solution)/shard_map/jit(cholesky)/cholesky | solution.py:51
  161.7 2.3 fusion.55
  164.3 2.6 convolution_subtract_fusion
  166.9 2.5 cholesky.240
  170.2 48.2 %custom-call.57 = f32[4,128,128]{2,1,0:T(8,128)S(1)} custom-call(f32[4,128,128]{2,1,0:T(8,128)} %cholesky.1020), custom_call_target="Cholesky" | custom-call | tf_op jit(solution)/shard_map/jit(cholesky)/cholesky | solution.py:51
  220.1 39.3 %custom-call.58 = f32[4,1,128,128]{2,3,1,0:T(8,128)S(1)} custom-call(f32[4,1,128,128]{3,2,1,0:T(8,128)S(1)} %get-tuple-element.45), custom_call_target="InvertDiagBlocksLowerTriangular" | custom-call | tf_op jit(solution)/shard_map/jit(cholesky)/cholesky | solution.py:51
  260.9 2.6 convolution_subtract_fusion.1
  263.6 46.9 %custom-call.59 = f32[4,128,128]{2,1,0:T(8,128)S(1)} custom-call(f32[4,128,128]{2,1,0:T(8,128)S(1)} %cholesky.1025), custom_call_target="Cholesky" | custom-call | tf_op jit(solution)/shard_map/jit(cholesky)/cholesky | solution.py:51
  311.3 39.5 %custom-call.60 = f32[4,1,128,128]{2,3,1,0:T(8,128)S(1)} custom-call(f32[4,1,128,128]{3,2,1,0:T(8,128)S(1)} %get-tuple-element.43), custom_call_target="InvertDiagBlocksLowerTriangular" | custom-call | tf_op jit(solution)/shard_map/jit(cholesky)/cholesky | solution.py:51
  351.9 2.6 convolution_subtract_fusion.10
  354.5 46.9 %custom-call.61 = f32[4,128,128]{2,1,0:T(8,128)S(1)} custom-call(f32[4,128,128]{2,1,0:T(8,128)S(1)} %convolution_subtract_fusion.10), custom_call_target="Cholesky" | custom-call | tf_op jit(solution)/shard_map/jit(cholesky)/cholesky | solution.py:51
  402.7 4.8 multiply_bitcast_fusion
  407.6 5.2 copy.145
  412.8 10.6 convolution_add_fusion
  428.7 23.5 %custom-call.83 = f32[2,128,128]{2,1,0:T(8,128)S(1)} custom-call(f32[2,128,128]{2,1,0:T(8,128)S(1)} %cholesky.1029), custom_call_target="Cholesky" | custom-call | tf_op jit(solution)/shard_map/jit(cholesky)/cholesky | solution.py:58
  453.1 21.1 %custom-call.84 = f32[2,1,128,128]{2,3,1,0:T(8,128)} custom-call(f32[2,1,128,128]{3,2,1,0:T(8,128)} %select_bitcast_fusion.15), custom_call_target="InvertDiagBlocksLowerTriangular" | custom-call | tf_op jit(solution)/shard_map/jit(cholesky)/cholesky | solution.py:58
  478.7 25.3 %custom-call.85 = f32[2,128,128]{2,1,0:T(8,128)} custom-call(f32[2,128,128]{2,1,0:T(8,128)} %cholesky.1033), custom_call_target="Cholesky" | custom-call | tf_op jit(solution)/shard_map/jit(cholesky)/cholesky | solution.py:58
  505.5 21.1 %custom-call.86 = f32[2,1,128,128]{2,3,1,0:T(8,128)} custom-call(f32[2,1,128,128]{3,2,1,0:T(8,128)} %get-tuple-element.65), custom_call_target="InvertDiagBlocksLowerTriangular" | custom-call | tf_op jit(solution)/shard_map/jit(cholesky)/cholesky | solution.py:58
  531.0 24.9 %custom-call.87 = f32[2,128,128]{2,1,0:T(8,128)} custom-call(f32[2,128,128]{2,1,0:T(8,128)} %cholesky.1038), custom_call_target="Cholesky" | custom-call | tf_op jit(solution)/shard_map/jit(cholesky)/cholesky | solution.py:58
  557.4 21.2 %custom-call.88 = f32[2,1,128,128]{2,3,1,0:T(8,128)} custom-call(f32[2,1,128,128]{3,2,1,0:T(8,128)} %get-tuple-element.63), custom_call_target="InvertDiagBlocksLowerTriangular" | custom-call | tf_op jit(solution)/shard_map/jit(cholesky)/cholesky | solution.py:58
  582.1 25.1 %custom-call.89 = f32[2,128,128]{2,1,0:T(8,128)} custom-call(f32[2,128,128]{2,1,0:T(8,128)} %convolution_subtract_fusion.14), custom_call_target="Cholesky" | custom-call | tf_op jit(solution)/shard_map/jit(cholesky)/cholesky | solution.py:58
  612.8 4.3 fusion.25
  617.1 15.9 %collective-permute-done.7 = f32[512,512]{0,1:T(8,128)S(1)} collective-permute-done((f32[512,512]{0,1:T(8,128)S(1)}, f32[512,512]{0,1:T(8,128)S(1)}, u32[]{:S(2)}, u32[]{:S(2)}) %collective-permute-start.7) | collective-permute-done | bytes 1048608 | tf_op jit(solution)/shard_map/ppermute | solution.py:39
  633.0 22.5 %collective-permute-done.8 = f32[512,512]{0,1:T(8,128)S(1)} collective-permute-done((f32[512,512]{0,1:T(8,128)S(1)}, f32[512,512]{0,1:T(8,128)S(1)}, u32[]{:S(2)}, u32[]{:S(2)}) %collective-permute-start.8) | collective-permute-done | bytes 1048608 | tf_op jit(solution)/shard_map/ppermute | solution.py:39
  655.5 3.5 add_add_fusion.2
  664.4 23.9 %custom-call.90 = f32[2,128,128]{2,1,0:T(8,128)S(1)} custom-call(f32[2,128,128]{2,1,0:T(8,128)S(1)} %cholesky.1042), custom_call_target="Cholesky" | custom-call | tf_op jit(solution)/shard_map/jit(cholesky)/cholesky | solution.py:71
  689.2 21.1 %custom-call.91 = f32[2,1,128,128]{2,3,1,0:T(8,128)} custom-call(f32[2,1,128,128]{3,2,1,0:T(8,128)} %select_bitcast_fusion.12), custom_call_target="InvertDiagBlocksLowerTriangular" | custom-call | tf_op jit(solution)/shard_map/jit(cholesky)/cholesky | solution.py:71
  714.7 24.9 %custom-call.92 = f32[2,128,128]{2,1,0:T(8,128)} custom-call(f32[2,128,128]{2,1,0:T(8,128)} %cholesky.1046), custom_call_target="Cholesky" | custom-call | tf_op jit(solution)/shard_map/jit(cholesky)/cholesky | solution.py:71
  741.2 21.2 %custom-call.93 = f32[2,1,128,128]{2,3,1,0:T(8,128)} custom-call(f32[2,1,128,128]{3,2,1,0:T(8,128)} %get-tuple-element.60), custom_call_target="InvertDiagBlocksLowerTriangular" | custom-call | tf_op jit(solution)/shard_map/jit(cholesky)/cholesky | solution.py:71
  766.8 24.9 %custom-call.94 = f32[2,128,128]{2,1,0:T(8,128)} custom-call(f32[2,128,128]{2,1,0:T(8,128)} %cholesky.1051), custom_call_target="Cholesky" | custom-call | tf_op jit(solution)/shard_map/jit(cholesky)/cholesky | solution.py:71
  793.2 21.1 %custom-call.95 = f32[2,1,128,128]{2,3,1,0:T(8,128)} custom-call(f32[2,1,128,128]{3,2,1,0:T(8,128)} %get-tuple-element.58), custom_call_target="InvertDiagBlocksLowerTriangular" | custom-call | tf_op jit(solution)/shard_map/jit(cholesky)/cholesky | solution.py:71
  817.7 25.1 %custom-call.96 = f32[2,128,128]{2,1,0:T(8,128)} custom-call(f32[2,128,128]{2,1,0:T(8,128)} %convolution_subtract_fusion.13), custom_call_target="Cholesky" | custom-call | tf_op jit(solution)/shard_map/jit(cholesky)/cholesky | solution.py:71
  845.7 13.3 collective-permute-start.9
  860.3 4.3 fusion.27
  864.5 15.5 %collective-permute-done.9 = f32[512,512]{0,1:T(8,128)S(1)} collective-permute-done((f32[512,512]{0,1:T(8,128)S(1)}, f32[512,512]{0,1:T(8,128)S(1)}, u32[]{:S(2)}, u32[]{:S(2)}) %collective-permute-start.9) | collective-permute-done | bytes 1048608 | tf_op jit(solution)/shard_map/ppermute | solution.py:39
  880.0 22.5 %collective-permute-done.10 = f32[512,512]{0,1:T(8,128)S(1)} collective-permute-done((f32[512,512]{0,1:T(8,128)S(1)}, f32[512,512]{0,1:T(8,128)S(1)}, u32[]{:S(2)}, u32[]{:S(2)}) %collective-permute-start.10) | collective-permute-done | bytes 1048608 | tf_op jit(solution)/shard_map/ppermute | solution.py:39
  902.5 3.5 add_add_fusion.1
  911.4 23.9 %custom-call.97 = f32[2,128,128]{2,1,0:T(8,128)S(1)} custom-call(f32[2,128,128]{2,1,0:T(8,128)S(1)} %cholesky.1055), custom_call_target="Cholesky" | custom-call | tf_op jit(solution)/shard_map/jit(cholesky)/cholesky | solution.py:71
  936.2 21.1 %custom-call.98 = f32[2,1,128,128]{2,3,1,0:T(8,128)} custom-call(f32[2,1,128,128]{3,2,1,0:T(8,128)} %select_bitcast_fusion.9), custom_call_target="InvertDiagBlocksLowerTriangular" | custom-call | tf_op jit(solution)/shard_map/jit(cholesky)/cholesky | solution.py:71
  961.7 24.9 %custom-call.99 = f32[2,128,128]{2,1,0:T(8,128)} custom-call(f32[2,128,128]{2,1,0:T(8,128)} %cholesky.1059), custom_call_target="Cholesky" | custom-call | tf_op jit(solution)/shard_map/jit(cholesky)/cholesky | solution.py:71
  988.2 21.2 %custom-call.100 = f32[2,1,128,128]{2,3,1,0:T(8,128)} custom-call(f32[2,1,128,128]{3,2,1,0:T(8,128)} %get-tuple-element.55), custom_call_target="InvertDiagBlocksLowerTriangular" | custom-call | tf_op jit(solution)/shard_map/jit(cholesky)/cholesky | solution.py:71
  1013.8 24.9 %custom-call.101 = f32[2,128,128]{2,1,0:T(8,128)} custom-call(f32[2,128,128]{2,1,0:T(8,128)} %cholesky.1064), custom_call_target="Cholesky" | custom-call | tf_op jit(solution)/shard_map/jit(cholesky)/cholesky | solution.py:71
  1040.3 21.1 %custom-call.102 = f32[2,1,128,128]{2,3,1,0:T(8,128)} custom-call(f32[2,1,128,128]{3,2,1,0:T(8,128)} %get-tuple-element.53), custom_call_target="InvertDiagBlocksLowerTriangular" | custom-call | tf_op jit(solution)/shard_map/jit(cholesky)/cholesky | solution.py:71
  1064.8 25.1 %custom-call.103 = f32[2,128,128]{2,1,0:T(8,128)} custom-call(f32[2,128,128]{2,1,0:T(8,128)} %convolution_subtract_fusion.12), custom_call_target="Cholesky" | custom-call | tf_op jit(solution)/shard_map/jit(cholesky)/cholesky | solution.py:71
  1096.4 4.3 fusion.29
  1100.7 67.8 %collective-permute-done.11 = f32[512,512]{0,1:T(8,128)} collective-permute-done((f32[512,512]{0,1:T(8,128)}, f32[512,512]{0,1:T(8,128)}, u32[]{:S(2)}, u32[]{:S(2)}) %collective-permute-start.11) | collective-permute-done | bytes 1048608 | tf_op jit(solution)/shard_map/ppermute | solution.py:39
  1168.5 22.5 %collective-permute-done.12 = f32[512,512]{0,1:T(8,128)} collective-permute-done((f32[512,512]{0,1:T(8,128)}, f32[512,512]{0,1:T(8,128)}, u32[]{:S(2)}, u32[]{:S(2)}) %collective-permute-start.12) | collective-permute-done | bytes 1048608 | tf_op jit(solution)/shard_map/ppermute | solution.py:39
  1191.0 5.8 add_add_fusion
  1202.2 23.9 %custom-call.104 = f32[2,128,128]{2,1,0:T(8,128)S(1)} custom-call(f32[2,128,128]{2,1,0:T(8,128)S(1)} %cholesky.1068), custom_call_target="Cholesky" | custom-call | tf_op jit(solution)/shard_map/jit(cholesky)/cholesky | solution.py:71
  1226.3 19.7 %custom-call.105 = f32[2,1,128,128]{2,3,1,0:T(8,128)S(1)} custom-call(f32[2,1,128,128]{3,2,1,0:T(8,128)S(1)} %select_bitcast_fusion.6), custom_call_target="InvertDiagBlocksLowerTriangular" | custom-call | tf_op jit(solution)/shard_map/jit(cholesky)/cholesky | solution.py:71
  1250.4 23.5 %custom-call.106 = f32[2,128,128]{2,1,0:T(8,128)S(1)} custom-call(f32[2,128,128]{2,1,0:T(8,128)S(1)} %cholesky.1072), custom_call_target="Cholesky" | custom-call | tf_op jit(solution)/shard_map/jit(cholesky)/cholesky | solution.py:71
  1274.0 19.8 %custom-call.107 = f32[2,1,128,128]{2,3,1,0:T(8,128)S(1)} custom-call(f32[2,1,128,128]{3,2,1,0:T(8,128)S(1)} %get-tuple-element.50), custom_call_target="InvertDiagBlocksLowerTriangular" | custom-call | tf_op jit(solution)/shard_map/jit(cholesky)/cholesky | solution.py:71
  1296.7 23.5 %custom-call.108 = f32[2,128,128]{2,1,0:T(8,128)S(1)} custom-call(f32[2,128,128]{2,1,0:T(8,128)S(1)} %cholesky.1077), custom_call_target="Cholesky" | custom-call | tf_op jit(solution)/shard_map/jit(cholesky)/cholesky | solution.py:71
  1320.2 19.7 %custom-call.109 = f32[2,1,128,128]{2,3,1,0:T(8,128)S(1)} custom-call(f32[2,1,128,128]{3,2,1,0:T(8,128)S(1)} %get-tuple-element.48), custom_call_target="InvertDiagBlocksLowerTriangular" | custom-call | tf_op jit(solution)/shard_map/jit(cholesky)/cholesky | solution.py:71
  1341.7 23.7 %custom-call.110 = f32[2,128,128]{2,1,0:T(8,128)S(1)} custom-call(f32[2,128,128]{2,1,0:T(8,128)S(1)} %convolution_subtract_fusion.11), custom_call_target="Cholesky" | custom-call | tf_op jit(solution)/shard_map/jit(cholesky)/cholesky | solution.py:71
  (213 shorter events, 140.8 us)
Async XLA Ops:
  8.8 11.8 copy-start.22
  8.8 11.8 copy-start.23
  8.8 14.3 %collective-permute-start = (bf16[2,128,256]{2,1,0:T(8,128)(2,1)}, bf16[2,128,256]{2,1,0:T(8,128)(2,1)}, u32[]{:S(2)}, u32[]{:S(2)}) collective-permute-start(bf16[2,128,256]{2,1,0:T(8,128)(2,1)} %get-tuple-element.40), channel_id=1, source_target_pairs={{0,1},{1,0},{2,3},{3,2},{4,5},{5,4},{6,7},{7,6},{8,9},{9,8},{10,11... | collective-permute-start | bytes 393224 | tf_op jit(solution)/shard_map/ppermute | solution.py:27
  10.9 17.1 %collective-permute-start.1 = (bf16[2,128,256]{2,1,0:T(8,128)(2,1)}, bf16[2,128,256]{2,1,0:T(8,128)(2,1)}, u32[]{:S(2)}, u32[]{:S(2)}) collective-permute-start(bf16[2,128,256]{2,1,0:T(8,128)(2,1)} %get-tuple-element.39), channel_id=1, source_target_pairs={{0,2},{1,3},{2,0},{3,1},{4,6},{5,7},{6,4},{7,5},{8,10},{9,11},{10,... | collective-permute-start | bytes 393224 | tf_op jit(solution)/shard_map/ppermute | solution.py:27
  12.2 18.5 %collective-permute-start.2 = (bf16[2,128,256]{2,1,0:T(8,128)(2,1)}, bf16[2,128,256]{2,1,0:T(8,128)(2,1)}, u32[]{:S(2)}, u32[]{:S(2)}) collective-permute-start(bf16[2,128,256]{2,1,0:T(8,128)(2,1)} %get-tuple-element.38), channel_id=1, source_target_pairs={{0,3},{1,2},{2,1},{3,0},{4,7},{5,6},{6,5},{7,4},{8,11},{9,10},{10,... | collective-permute-start | bytes 393224 | tf_op jit(solution)/shard_map/ppermute | solution.py:27
  12.2 20.1 %collective-permute-start.3 = (bf16[2,128,256]{2,1,0:T(8,128)(2,1)}, bf16[2,128,256]{2,1,0:T(8,128)(2,1)}, u32[]{:S(2)}, u32[]{:S(2)}) collective-permute-start(bf16[2,128,256]{2,1,0:T(8,128)(2,1)} %get-tuple-element.37), channel_id=1, source_target_pairs={{0,4},{1,5},{2,6},{3,7},{4,0},{5,1},{6,2},{7,3},{8,12},{9,13},{10,... | collective-permute-start | bytes 393224 | tf_op jit(solution)/shard_map/ppermute | solution.py:27
  14.6 19.2 %collective-permute-start.4 = (bf16[2,128,256]{2,1,0:T(8,128)(2,1)}, bf16[2,128,256]{2,1,0:T(8,128)(2,1)}, u32[]{:S(2)}, u32[]{:S(2)}) collective-permute-start(bf16[2,128,256]{2,1,0:T(8,128)(2,1)} %get-tuple-element.36), channel_id=1, source_target_pairs={{0,5},{1,4},{2,7},{3,6},{4,1},{5,0},{6,3},{7,2},{8,13},{9,12},{10,... | collective-permute-start | bytes 393224 | tf_op jit(solution)/shard_map/ppermute | solution.py:27
  15.6 39.8 %all-to-all-start = ((bf16[16,128,256]{2,1,0:T(8,128)(2,1)}), bf16[16,128,256]{2,1,0:T(8,128)(2,1)}, u32[]{:S(2)}, u32[]{:S(2)}) async-start(bf16[16,128,256]{2,1,0:T(8,128)(2,1)} %param.12), calls=%async_computation | async-start | bytes 2097152 | tf_op jit(solution)/shard_map/all_to_all | solution.py:77
  20.2 1.0 copy-start.21
  20.2 1350.0 %all-gather.2.cloned.1.call-start = ((), (), s32[]{:S(2)}) async-start(), calls=%async_computation.1 | async-start | bytes 1179648 | tf_op jit(solution)/shard_map/all_gather | solution.py:101
  20.4 380.9 %copy-start.16 = (pred[128,128]{1,0:T(8,128)(4,1)}, pred[128,128]{1,0:T(8,128)(4,1)S(1)}, u32[]{:S(2)}) copy-start(pred[128,128]{1,0:T(8,128)(4,1)S(1)} %iota_compare_fusion.3) | copy-start | bytes 49156
  23.1 22.3 %collective-permute-start.5 = (bf16[2,128,256]{2,1,0:T(8,128)(2,1)}, bf16[2,128,256]{2,1,0:T(8,128)(2,1)S(1)}, u32[]{:S(2)}, u32[]{:S(2)}) collective-permute-start(bf16[2,128,256]{2,1,0:T(8,128)(2,1)} %get-tuple-element.35), channel_id=1, source_target_pairs={{0,6},{1,7},{2,4},{3,5},{4,2},{5,3},{6,0},{7,1},{8,14},{9,15},{10,... | collective-permute-start | bytes 393224 | tf_op jit(solution)/shard_map/ppermute | solution.py:27
  27.9 19.8 %collective-permute-start.6 = (bf16[2,128,256]{2,1,0:T(8,128)(2,1)}, bf16[2,128,256]{2,1,0:T(8,128)(2,1)S(1)}, u32[]{:S(2)}, u32[]{:S(2)}) collective-permute-start(bf16[2,128,256]{2,1,0:T(8,128)(2,1)} %get-tuple-element.34), channel_id=1, source_target_pairs={{0,7},{1,6},{2,5},{3,4},{4,3},{5,2},{6,1},{7,0},{8,15},{9,14},{10,... | collective-permute-start | bytes 393224 | tf_op jit(solution)/shard_map/ppermute | solution.py:27
  51.3 1.5 copy-start.15
  55.4 1.9 copy-start.7
  73.5 1.9 copy-start
  166.9 2.5 copy-start.5
  170.2 89.3 %copy-start.6 = (f32[4,384,128]{2,1,0:T(8,128)S(1)}, f32[4,384,128]{2,1,0:T(8,128)}, u32[]{:S(2)}) copy-start(f32[4,384,128]{2,1,0:T(8,128)} %copy-done.5) | copy-start | bytes 2359300
  427.4 1.4 copy-start.2
  477.3 0.8 copy-start.9
  529.6 0.7 copy-start.12
  609.8 3.0 copy-start.18
  610.0 23.0 %collective-permute-start.7 = (f32[512,512]{0,1:T(8,128)S(1)}, f32[512,512]{0,1:T(8,128)S(1)}, u32[]{:S(2)}, u32[]{:S(2)}) collective-permute-start(f32[512,512]{0,1:T(8,128)S(1)} %get-tuple-element.32), channel_id=1, source_target_pairs={{0,1},{1,0},{2,3},{3,2},{4,5},{5,4},{6,7},{7,6},{8,9},{9,8},{10,11... | collective-permute-start | bytes 3145736 | tf_op jit(solution)/shard_map/ppermute | solution.py:39
  611.0 44.5 %collective-permute-start.8 = (f32[512,512]{0,1:T(8,128)S(1)}, f32[512,512]{0,1:T(8,128)S(1)}, u32[]{:S(2)}, u32[]{:S(2)}) collective-permute-start(f32[512,512]{0,1:T(8,128)S(1)} %get-tuple-element.33), channel_id=1, source_target_pairs={{0,1},{1,0},{2,3},{3,2},{4,5},{5,4},{6,7},{7,6},{8,9},{9,8},{10,11... | collective-permute-start | bytes 3145736 | tf_op jit(solution)/shard_map/ppermute | solution.py:39
  663.0 1.4 copy-start.3
  713.3 0.8 copy-start.10
  765.4 0.7 copy-start.13
  845.5 14.8 %copy-start.20 = (f32[512]{0:T(512)S(1)}, f32[512]{0:T(512)}, u32[]{:S(2)}) copy-start(f32[512]{0:T(512)} %fusion.121) | copy-start | bytes 6148
  845.7 34.4 %collective-permute-start.9 = (f32[512,512]{0,1:T(8,128)S(1)}, f32[512,512]{0,1:T(8,128)S(1)}, u32[]{:S(2)}, u32[]{:S(2)}) collective-permute-start(f32[512,512]{0,1:T(8,128)S(1)} %get-tuple-element.30), channel_id=1, source_target_pairs={{0,2},{2,0},{1,3},{3,1},{4,6},{6,4},{5,7},{7,5},{8,10},{10,8},{9,1... | collective-permute-start | bytes 3145736 | tf_op jit(solution)/shard_map/ppermute | solution.py:39
  859.0 43.5 %collective-permute-start.10 = (f32[512,512]{0,1:T(8,128)S(1)}, f32[512,512]{0,1:T(8,128)S(1)}, u32[]{:S(2)}, u32[]{:S(2)}) collective-permute-start(f32[512,512]{0,1:T(8,128)S(1)} %get-tuple-element.31), channel_id=1, source_target_pairs={{0,2},{2,0},{1,3},{3,1},{4,6},{6,4},{5,7},{7,5},{8,10},{10,8},{9,1... | collective-permute-start | bytes 3145736 | tf_op jit(solution)/shard_map/ppermute | solution.py:39
  910.0 1.4 copy-start.4
  960.3 0.8 copy-start.11
  1012.4 0.7 copy-start.14
  1092.5 3.9 copy-start.19
  1094.0 74.5 %collective-permute-start.11 = (f32[512,512]{0,1:T(8,128)}, f32[512,512]{0,1:T(8,128)}, u32[]{:S(2)}, u32[]{:S(2)}) collective-permute-start(f32[512,512]{0,1:T(8,128)} %get-tuple-element.28), channel_id=1, source_target_pairs={{0,4},{4,0},{1,5},{5,1},{2,6},{6,2},{3,7},{7,3},{8,12},{12,8},{9,1... | collective-permute-start | bytes 3145736 | tf_op jit(solution)/shard_map/ppermute | solution.py:39
  1096.0 95.0 %collective-permute-start.12 = (f32[512,512]{0,1:T(8,128)}, f32[512,512]{0,1:T(8,128)}, u32[]{:S(2)}, u32[]{:S(2)}) collective-permute-start(f32[512,512]{0,1:T(8,128)} %get-tuple-element.29), channel_id=1, source_target_pairs={{0,4},{4,0},{1,5},{5,1},{2,6},{6,2},{3,7},{7,3},{8,12},{12,8},{9,1... | collective-permute-start | bytes 3145736 | tf_op jit(solution)/shard_map/ppermute | solution.py:39
  1200.8 1.4 copy-start.1
  1249.7 0.7 copy-start.8
  1273.9 91.5 %copy-start.17 = (pred[128,128]{1,0:T(8,128)(4,1)S(1)}, pred[128,128]{1,0:T(8,128)(4,1)}, u32[]{:S(2)}) copy-start(pred[128,128]{1,0:T(8,128)(4,1)} %copy-done.16) | copy-start | bytes 49156
  1367.5 4.8 collective-permute-start.13
Sparse Core Ops, SparseCore 0:
  1096.5 114.2 all-gather.1
